TPU v7x, 512 devices: a whole 4x4x16 slice. The times are simulated.
512 devices in a mesh: dp: 128 (over x, z, core), tensor: 4 (over y).
Axes of the slice: x: 4, y: 4, z: 16, core: 2. Of those that a mesh axis runs over, the one named last changes fastest.
Arguments:
- tokens: bfloat16 [32768, 2048], P('dp', 'tensor'), may hold values from -6 to 6
- expert_ids: int32 [32768, 2], P('dp'), may hold values from 0 to 127, as said below
- route_weights: float32 [32768, 2], P('dp'), may hold values from 0.2 to 1
- gate_weight: bfloat16 [128, 2048, 1024], P('dp', None, 'tensor'), may hold values from -0.125 to 0.125
- up_weight: bfloat16 [128, 2048, 1024], P('dp', None, 'tensor'), may hold values from -0.125 to 0.125
- down_weight: bfloat16 [128, 1024, 2048], P('dp', 'tensor'), may hold values from -0.1875 to 0.1875
Outputs:
- moe_out: bfloat16 [32768, 2048], P('dp', 'tensor')
Inputs may be any that keep to these rules, and one draw needn't show every extreme that they name: `expert_ids`: the two experts of a row differ. Among the rows of one index of dp, no expert is named more than 8 times.
All inputs are finite; a program needn't handle non-finite values.
Results may differ from a plain program's by a relative error of at most 0.011.
Values may be sent and summed in bfloat16 or wider, within the bound.
A program may use at most 64 MiB of HBM per device.

v0:
```python
import jax
import jax.numpy as jnp
from jax import lax
from jax.sharding import PartitionSpec as P


def body(tokens, expert_ids, route_weights, gate_weight, up_weight, down_weight):
    tok_count = tokens.shape[0]
    local_experts = gate_weight.shape[0]
    model_width = gate_weight.shape[1]
    groups = lax.axis_size("dp")
    experts_all = local_experts * groups
    capacity = 4 * tok_count // groups
    chosen = expert_ids.reshape(-1)
    onehot = (chosen[:, None] == jnp.arange(experts_all, dtype=jnp.int32)[None, :]).astype(
        jnp.int32
    )
    earlier = jnp.cumsum(onehot, axis=0) - onehot
    slot_index = jnp.sum(earlier * onehot, axis=1)
    flat_slot = chosen * capacity + slot_index
    source_rows = tokens[jnp.arange(chosen.shape[0], dtype=jnp.int32) // 2]
    send_buffer = (
        jnp.zeros((experts_all * capacity, tokens.shape[1]), jnp.bfloat16)
        .at[flat_slot]
        .set(source_rows)
    )
    send_buffer = send_buffer.reshape(experts_all, 1, capacity, tokens.shape[1])
    features = lax.all_gather(
        lax.all_to_all(send_buffer, "dp", split_axis=0, concat_axis=1, tiled=True),
        "tensor",
        axis=3,
        tiled=True,
    )
    slot_count = features.shape[2]
    token_rows = features[0].reshape(-1, model_width)
    gate_value = jnp.dot(token_rows, gate_weight[0], preferred_element_type=jnp.float32)
    up_value = jnp.dot(token_rows, up_weight[0], preferred_element_type=jnp.float32)
    hidden = (jax.nn.silu(gate_value) * up_value).astype(jnp.bfloat16)
    partial_sum = jnp.dot(hidden, down_weight[0], preferred_element_type=jnp.float32)
    results = [partial_sum.reshape(features.shape[1], slot_count, model_width)]
    partial_out = jnp.stack(results, axis=0)
    reduced = lax.psum_scatter(
        partial_out.astype(jnp.bfloat16), "tensor", scatter_dimension=3, tiled=True
    )
    came_back = lax.all_to_all(reduced, "dp", split_axis=1, concat_axis=0, tiled=True)
    quarter_width = came_back.shape[3]
    result_table = came_back.reshape(experts_all * capacity, quarter_width)
    picked = result_table[flat_slot].astype(jnp.float32).reshape(tok_count, 2, quarter_width)
    mixed_out = jnp.sum(picked * route_weights[:, :, None], axis=1)
    return mixed_out.astype(jnp.bfloat16)


def solution(mesh):
    return jax.shard_map(
        body,
        mesh=mesh,
        in_specs=(
            P("dp", "tensor"),
            P("dp", None),
            P("dp", None),
            P("dp", None, "tensor"),
            P("dp", None, "tensor"),
            P("dp", "tensor", None),
        ),
        out_specs=P("dp", "tensor"),
        check_vma=False,
    )
```

profile of v0, /device:TPU:2, one launch (start us, length us, event | category | flops | bytes accessed | tf_op | source)
XLA Modules:
  0.0 289.4 jit_solution(14001448226767223536)
XLA Ops:
  6.5 1.0 copy.18
  7.5 0.1 eq.29
  7.7 0.1 eq.25
  7.8 0.7 broadcast_multiply_fusion
  8.5 0.1 copy.20
  8.6 0.2 fusion.22
  8.9 0.1 copy.17
  9.1 0.1 mul.36
  9.2 0.2 fusion.21
  9.5 6.4 %scatter_custom_fusion = bf16[1024,512]{1,0:T(8,128)(2,1)S(1)} fusion(s32[512]{0:T(512)S(1)} %bitcast.49, bf16[256,512]{1,0:T(8,128)(2,1)} %param.6, s32[1024]{0:T(1024)S(1)} %pad_clamp_fusion.1, bf16[]{:T(256)} %constant.26.clone.1), kind=kCustom, calls=%fused_computation.16 | custom fusion | bytes 1049088 | tf_op jit(solution)/shard_map/scatter | solution.py:25
  15.9 75.5 %all_to_all.21 = bf16[128,1,8,512]{3,2,1,0:T(8,128)(2,1)} all-to-all(bf16[128,1,8,512]{3,2,1,0:T(8,128)(2,1)S(1)} %bitcast.44), channel_id=1, replica_groups=mesh['dp'=128,'tensor'=4] {'dp'}, dimensions={0} | all-to-all | bytes 2097152 | tf_op jit(solution)/shard_map/all_to_all | solution.py:29
  91.4 0.2 reduce-scatter.2.cloned.1.call-start
  91.7 47.5 %all-gather.3.cloned.1.call-done = bf16[128,1,8,2048]{3,2,1,0:T(8,128)(2,1)} async-done(((bf16[128,1,8,512]{3,2,1,0:T(8,128)(2,1)}), bf16[128,1,8,2048]{3,2,1,0:T(8,128)(2,1)}) %all-gather.3.cloned.1.call-update) | async-done | bytes 4194320 | tf_op jit(solution)/shard_map/all_gather | solution.py:28
  139.2 3.6 %fusion.2 = f32[1024,256]{1,0:T(8,128)S(1)} fusion(bf16[128,1,8,2048]{3,2,1,0:T(8,128)(2,1)} %all-gather.3.cloned.1.call-done, bf16[1,2048,256]{2,1,0:T(8,128)(2,1)S(1)} %copy-done.3), kind=kOutput, calls=%fused_computation.5 | convolution fusion | flops 1073741824 | bytes 6291456 | tf_op jit(solution)/shard_map/dot_general | solution.py:36
  142.8 1.3 fusion.10
  144.1 3.2 %convert_bitcast_fusion = bf16[1,128,8,2048]{3,1,2,0:T(8,128)(2,1)} fusion(bf16[1,256,2048]{2,1,0:T(8,128)(2,1)S(1)} %copy-done, bf16[128,8,256]{2,1,0:T(8,128)(2,1)S(1)} %fusion.10), kind=kOutput, calls=%fused_computation.7 | convolution fusion | flops 1075838976 | bytes 5767168 | tf_op jit(solution)/shard_map/dot_general | solution.py:39
  147.4 55.1 %reduce-scatter.2.cloned.1.call-done = bf16[1,128,8,512]{3,1,2,0:T(8,128)(2,1)} async-done(((bf16[1,128,8,2048]{3,1,2,0:T(8,128)(2,1)}), bf16[1,128,8,512]{3,1,2,0:T(8,128)(2,1)}) %reduce-scatter.2.cloned.1.call-update) | async-done | bytes 1048592 | tf_op jit(solution)/shard_map/reduce_scatter | solution.py:42
  202.4 2.8 copy.23
  205.2 16.6 %all-to-all-start.1 = ((bf16[1,128,8,512]{3,2,0,1:T(8,128)(2,1)}), bf16[1,128,8,512]{3,2,0,1:T(8,128)(2,1)S(1)}, u32[]{:S(2)}, u32[]{:S(2)}) async-start(bf16[1,128,8,512]{3,2,0,1:T(8,128)(2,1)} %copy.23), calls=%async_computation.2 | async-start | bytes 2097152 | tf_op jit(solution)/shard_map/all_to_all | solution.py:45
  221.8 0.1 copy.24
  222.0 55.9 %all-to-all-done.1 = bf16[1,128,8,512]{3,2,0,1:T(8,128)(2,1)S(1)} async-done(((bf16[1,128,8,512]{3,2,0,1:T(8,128)(2,1)}), bf16[1,128,8,512]{3,2,0,1:T(8,128)(2,1)S(1)}, u32[]{:S(2)}, u32[]{:S(2)}) %all-to-all-start.1) | async-done | bytes 1048608 | tf_op jit(solution)/shard_map/all_to_all | solution.py:45
  277.9 2.0 gather_fusion
  279.9 0.7 reshape.113
  280.5 2.1 multiply_reduce_fusion
  (23 shorter events, 0.2 us)
Async XLA Ops:
  6.5 137.6 %copy-start = (bf16[1,256,2048]{2,1,0:T(8,128)(2,1)S(1)}, bf16[1,256,2048]{2,1,0:T(8,128)(2,1)}, u32[]{:S(2)}) copy-start(bf16[1,256,2048]{2,1,0:T(8,128)(2,1)} %param.11) | copy-start | bytes 3145732
  6.5 132.7 %copy-start.3 = (bf16[1,2048,256]{2,1,0:T(8,128)(2,1)S(1)}, bf16[1,2048,256]{2,1,0:T(8,128)(2,1)}, u32[]{:S(2)}) copy-start(bf16[1,2048,256]{2,1,0:T(8,128)(2,1)} %param.9) | copy-start | bytes 3145732
  6.5 132.7 %all-gather.3.cloned.1.call-start = ((), (), s32[]{:S(2)}) async-start(), calls=%async_computation.4 | async-start | bytes 5242880 | tf_op jit(solution)/shard_map/all_gather | solution.py:28
  91.4 51.4 %copy-start.4 = (bf16[1,2048,256]{2,1,0:T(8,128)(2,1)S(1)}, bf16[1,2048,256]{2,1,0:T(8,128)(2,1)}, u32[]{:S(2)}) copy-start(bf16[1,2048,256]{2,1,0:T(8,128)(2,1)} %param.10) | copy-start | bytes 3145732
  91.4 111.0 %reduce-scatter.2.cloned.1.call-start = ((), (), s32[]{:S(2)}) async-start(), calls=%async_computation.3 | async-start | bytes 5242880 | tf_op jit(solution)/shard_map/reduce_scatter | solution.py:42
  139.2 3.6 %copy-start.2 = (bf16[128,1,8,2048]{3,2,1,0:T(8,128)(2,1)S(1)}, bf16[128,1,8,2048]{3,2,1,0:T(8,128)(2,1)}, u32[]{:S(2)}) copy-start(bf16[128,1,8,2048]{3,2,1,0:T(8,128)(2,1)} %all-gather.3.cloned.1.call-done) | copy-start | bytes 12582916
  147.3 74.5 %copy-start.1 = (f32[256,2]{0,1:T(2,128)S(1)}, f32[256,2]{0,1:T(2,128)}, u32[]{:S(2)}) copy-start(f32[256,2]{0,1:T(2,128)} %param.8) | copy-start | bytes 6148
  205.2 72.7 %all-to-all-start.1 = ((bf16[1,128,8,512]{3,2,0,1:T(8,128)(2,1)}), bf16[1,128,8,512]{3,2,0,1:T(8,128)(2,1)S(1)}, u32[]{:S(2)}, u32[]{:S(2)}) async-start(bf16[1,128,8,512]{3,2,0,1:T(8,128)(2,1)} %copy.23), calls=%async_computation.2 | async-start | bytes 2097152 | tf_op jit(solution)/shard_map/all_to_all | solution.py:45
Sparse Core Ops, SparseCore 0:
  91.6 47.6 all-gather.2
  147.5 54.8 reduce-scatter.1
where the time goes:
time: 290 us; the launch traced here: 289 us
  waiting for transfers between devices  159 us (55%)
  blocking collectives  75.5 us (26%)
  starting transfers between devices  16.8 us (6%)
  local copies, waits for them, and re-layouts  13.6 us (5%)
  between operations  13.6 us (5%)
  matrix products  8.07 us (3%)
  other arithmetic  3.26 us (1%)
    all_to_all x1, blocking collectives, body(): lax.all_to_all(send_buffer, 'dp', split_axis=0, concat_axis=1, tiled=True)  75.5 us
    all_to_all x1, waiting for transfers between devices, body(): lax.all_to_all(reduced, 'dp', split_axis=1, concat_axis=0, tiled=True)  55.9 us
    reduce_scatter x1, waiting for transfers between devices, body(): lax.psum_scatter(partial_out.astype(jnp.bfloat16), 'tensor', scatter_dime...  55.1 us
    all_gather x1, waiting for transfers between devices, body(): lax.all_gather(lax.all_to_all(send_buffer, 'dp', split_axis=0, concat_axi...  47.5 us
    all_to_all x1, starting transfers between devices, body(): lax.all_to_all(reduced, 'dp', split_axis=1, concat_axis=0, tiled=True)  16.6 us
    scatter x1, local copies, waits for them, and re-layouts, body(): send_buffer = jnp.zeros((experts_all * capacity, tokens.shape[1]), jnp.bf...  6.4 us
  transfers between devices with their start and end apart: 3, of which 3 were waited for; matrix products, arithmetic and copies ran while one was open for 0% of the time, Pallas kernels for 0%

commit v1 on v0

--- a/solution.py
+++ b/solution.py
@@ -25,12 +25,11 @@
         .set(source_rows)
     )
     send_buffer = send_buffer.reshape(experts_all, 1, capacity, tokens.shape[1])
-    features = lax.all_gather(
-        lax.all_to_all(send_buffer, "dp", split_axis=0, concat_axis=1, tiled=True),
-        "tensor",
-        axis=3,
-        tiled=True,
-    )
+    block = lax.all_to_all(send_buffer, "dp", split_axis=0, concat_axis=1, tiled=True)
+    size = lax.axis_size("tensor")
+    blocks = jnp.stack([block for _ in range(size)])
+    blocks = lax.all_to_all(blocks, "tensor", split_axis=0, concat_axis=0)
+    features = jnp.concatenate(blocks, axis=3)
     slot_count = features.shape[2]
     token_rows = features[0].reshape(-1, model_width)
     gate_value = jnp.dot(token_rows, gate_weight[0], preferred_element_type=jnp.float32)

time: 290 us -> 289 us (level)
  waiting for transfers between devices: 159 us -> 102 us
  blocking collectives: 75.5 us -> 127 us
  local copies, waits for them, and re-layouts: 13.6 us -> 20.7 us
    all_to_all x0 -> x1, blocking collectives: none -> 51.3 us  [body(): blocks = lax.all_to_all(blocks, 'tensor', split_axis=0, concat_axis=0)]
    all_gather x1 -> x0, waiting for transfers between devices: 47.5 us -> none  [body(): lax.all_gather(lax.all_to_all(send_buffer, 'dp', split_axis=0, concat_axi...]
    reduce_scatter x1, waiting for transfers between devices: 55.1 us -> 46 us  [body(): lax.psum_scatter(partial_out.astype(jnp.bfloat16), 'tensor', scatter_dime...]
    reshape x0 -> x1, local copies, waits for them, and re-layouts: none -> 5.39 us  [body(): features = jnp.concatenate(blocks, axis=3)]
  transfers between devices with their start and end apart: 3 -> 2, of which waited for: 3 -> 2; matrix products, arithmetic and copies ran while one was open for 0% -> 0% of each run, Pallas kernels for 0% -> 0%
where the time goes in v1:
time: 289 us
  blocking collectives  127 us (44%)
  waiting for transfers between devices  102 us (35%)
  local copies, waits for them, and re-layouts  20.7 us (7%)
  starting transfers between devices  16.6 us (6%)
  between operations  13.6 us (5%)
  matrix products  5.75 us (2%)
  other arithmetic  3.26 us (1%)
    all_to_all x1, blocking collectives, body(): lax.all_to_all(send_buffer, 'dp', split_axis=0, concat_axis=1, tiled=True)  75.4 us
    all_to_all x1, waiting for transfers between devices, body(): lax.all_to_all(reduced, 'dp', split_axis=1, concat_axis=0, tiled=True)  55.9 us
    all_to_all x1, blocking collectives, body(): blocks = lax.all_to_all(blocks, 'tensor', split_axis=0, concat_axis=0)  51.3 us
    reduce_scatter x1, waiting for transfers between devices, body(): lax.psum_scatter(partial_out.astype(jnp.bfloat16), 'tensor', scatter_dime...  46 us
    all_to_all x1, starting transfers between devices, body(): lax.all_to_all(reduced, 'dp', split_axis=1, concat_axis=0, tiled=True)  16.6 us
    scatter x1, local copies, waits for them, and re-layouts, body(): send_buffer = jnp.zeros((experts_all * capacity, tokens.shape[1]), jnp.bf...  6.4 us
  transfers between devices with their start and end apart: 2, of which 2 were waited for; matrix products, arithmetic and copies ran while one was open for 0% of the time, Pallas kernels for 0%

profile of v1, /device:TPU:2, one launch (start us, length us, event | category | flops | bytes accessed | tf_op | source)
XLA Modules:
  0.0 288.5 jit_solution(9912662370453579189)
XLA Ops:
  6.5 0.9 copy.18
  7.4 0.1 eq.29
  7.6 0.1 eq.25
  7.7 0.7 broadcast_multiply_fusion
  8.5 0.2 fusion.12
  8.9 0.1 copy.17
  9.0 0.1 mul.36
  9.2 0.2 fusion.11
  9.4 6.4 %scatter_custom_fusion = bf16[1024,512]{1,0:T(8,128)(2,1)S(1)} fusion(s32[512]{0:T(512)S(1)} %bitcast.52, bf16[256,512]{1,0:T(8,128)(2,1)} %param.6, s32[1024]{0:T(1024)S(1)} %pad_clamp_fusion.1, bf16[]{:T(256)} %constant.26.clone.1), kind=kCustom, calls=%fused_computation.14 | custom fusion | bytes 1049088 | tf_op jit(solution)/shard_map/scatter | solution.py:25
  15.8 75.4 %all_to_all.23 = bf16[128,1,8,512]{3,2,1,0:T(8,128)(2,1)S(1)} all-to-all(bf16[128,1,8,512]{3,2,1,0:T(8,128)(2,1)S(1)} %bitcast.47), channel_id=1, replica_groups=mesh['dp'=128,'tensor'=4] {'dp'}, dimensions={0} | all-to-all | bytes 2097152 | tf_op jit(solution)/shard_map/all_to_all | solution.py:28
  91.2 0.3 stack.10
  91.6 51.3 %all_to_all.24 = bf16[4,1,128,8,512]{4,3,2,1,0:T(8,128)(2,1)S(1)} all-to-all(bf16[4,1,128,8,512]{4,3,2,1,0:T(8,128)(2,1)S(1)} %stack.10), channel_id=1, replica_groups=mesh['dp'=128,'tensor'=4] {'tensor'}, dimensions={0} | all-to-all | bytes 8388608 | tf_op jit(solution)/shard_map/all_to_all | solution.py:31
  142.8 5.4 %copy.30 = bf16[1,128,8,4,512]{4,3,2,1,0:T(4,128)(2,1)S(1)} copy(bf16[1,128,8,4,512]{4,2,1,0,3:T(8,128)(2,1)S(1)} %bitcast.42) | data formatting | bytes 8388608 | tf_op jit(solution)/shard_map/reshape | solution.py:32
  148.2 1.4 copy.26
  149.7 1.3 fusion.4
  150.9 1.3 fusion.1
  152.3 3.2 %convert_bitcast_fusion = bf16[1,128,8,2048]{3,1,2,0:T(8,128)(2,1)} fusion(bf16[1,256,2048]{2,1,0:T(8,128)(2,1)S(1)} %copy-done, bf16[128,8,256]{2,1,0:T(8,128)(2,1)S(1)} %fusion.1), kind=kOutput, calls=%fused_computation.4 | convolution fusion | flops 1075838976 | bytes 5767168 | tf_op jit(solution)/shard_map/dot_general | solution.py:38
  155.5 46.0 %reduce-scatter.2.cloned.1.call-done = bf16[1,128,8,512]{3,1,2,0:T(8,128)(2,1)} async-done(((bf16[1,128,8,2048]{3,1,2,0:T(8,128)(2,1)}), bf16[1,128,8,512]{3,1,2,0:T(8,128)(2,1)}) %reduce-scatter.2.cloned.1.call-update) | async-done | bytes 1048592 | tf_op jit(solution)/shard_map/reduce_scatter | solution.py:41
  201.5 2.8 copy.24
  204.3 16.6 %all-to-all-start.2 = ((bf16[1,128,8,512]{3,2,0,1:T(8,128)(2,1)}), bf16[1,128,8,512]{3,2,0,1:T(8,128)(2,1)S(1)}, u32[]{:S(2)}, u32[]{:S(2)}) async-start(bf16[1,128,8,512]{3,2,0,1:T(8,128)(2,1)} %copy.24), calls=%async_computation.3 | async-start | bytes 2097152 | tf_op jit(solution)/shard_map/all_to_all | solution.py:44
  221.0 55.9 %all-to-all-done.2 = bf16[1,128,8,512]{3,2,0,1:T(8,128)(2,1)S(1)} async-done(((bf16[1,128,8,512]{3,2,0,1:T(8,128)(2,1)}), bf16[1,128,8,512]{3,2,0,1:T(8,128)(2,1)S(1)}, u32[]{:S(2)}, u32[]{:S(2)}) %all-to-all-start.2) | async-done | bytes 1048608 | tf_op jit(solution)/shard_map/all_to_all | solution.py:44
  277.0 2.0 gather_fusion
  278.9 0.7 reshape.122
  279.6 2.1 multiply_reduce_fusion
  (22 shorter events, 0.4 us)
Async XLA Ops:
  6.5 145.7 %copy-start = (bf16[1,256,2048]{2,1,0:T(8,128)(2,1)S(1)}, bf16[1,256,2048]{2,1,0:T(8,128)(2,1)}, u32[]{:S(2)}) copy-start(bf16[1,256,2048]{2,1,0:T(8,128)(2,1)} %param.11) | copy-start | bytes 3145732
  6.5 195.0 %reduce-scatter.2.cloned.1.call-start = ((), (), s32[]{:S(2)}) async-start(), calls=%async_computation.4 | async-start | bytes 5242880 | tf_op jit(solution)/shard_map/reduce_scatter | solution.py:41
  148.2 1.4 copy-start.2
  149.7 1.3 copy-start.3
  155.5 65.4 %copy-start.1 = (f32[256,2]{0,1:T(2,128)S(1)}, f32[256,2]{0,1:T(2,128)}, u32[]{:S(2)}) copy-start(f32[256,2]{0,1:T(2,128)} %param.8) | copy-start | bytes 6148
  204.3 72.7 %all-to-all-start.2 = ((bf16[1,128,8,512]{3,2,0,1:T(8,128)(2,1)}), bf16[1,128,8,512]{3,2,0,1:T(8,128)(2,1)S(1)}, u32[]{:S(2)}, u32[]{:S(2)}) async-start(bf16[1,128,8,512]{3,2,0,1:T(8,128)(2,1)} %copy.24), calls=%async_computation.3 | async-start | bytes 2097152 | tf_op jit(solution)/shard_map/all_to_all | solution.py:44
Sparse Core Ops, SparseCore 0:
  155.6 45.8 reduce-scatter.1
